TPU v7x, 512 devices: a whole 4x8x8 slice. The times are simulated.
512 devices in a mesh: ctx: 32 (over z, y_hi, core), tp: 16 (over x, y_lo).
Axes of the slice: x: 4, y: 8 (y_hi: 2, y_lo: 4; y = y_hi * 4 + y_lo), z: 8, core: 2. Of those that a mesh axis runs over, the one named last changes fastest.
Arguments:
- q_proj: bfloat16 [4096, 4096], P('ctx', 'tp'), may hold values from -6 to 6
- k_proj: bfloat16 [4096, 4096], P('ctx', 'tp'), may hold values from -6 to 6
- v_proj: bfloat16 [4096, 4096], P('ctx', 'tp'), may hold values from -6 to 6
- saved_conv: bfloat16 [4096, 4096], P('ctx', 'tp'), may hold values from -6 to 6
- out_grad: bfloat16 [4096, 4096], P('ctx', 'tp'), may hold values from -6 to 6
- out_weight: bfloat16 [4096, 4096], P('tp'), may hold values from -0.09375 to 0.09375
- filter_taps: bfloat16 [4096, 4096], P('ctx', 'tp'), may hold values from -1.1 to 1.1
Outputs:
- dq_grad: bfloat16 [4096, 4096], P('ctx', 'tp')
- dk_grad: bfloat16 [4096, 4096], P('ctx', 'tp')
- dv_grad: bfloat16 [4096, 4096], P('ctx', 'tp')
- filter_grad: float32 [4096, 4096], P('ctx', 'tp')
All inputs are finite; a program needn't handle non-finite values.
Results may differ from a plain program's by a relative error of at most 0.003.
Values may be sent and summed in bfloat16 or wider, within the bound.
A program may use at most 128 MiB of HBM per device.

v0:
```python
import math
import jax
import jax.numpy as jnp
from jax import lax
from jax.sharding import PartitionSpec as P


def from_behind(value, axis, steps):
    count = lax.axis_size(axis)
    pairs = [(source, (source + steps) % count) for source in range(count)]
    return lax.ppermute(value, axis, pairs)


def passed_along(block, axis, distance):
    devices = range(lax.axis_size(axis))
    route = [(i - distance, i) for i in devices if i - distance in devices]
    return lax.ppermute(block, axis, route)


def matmul(left, right):
    return jnp.dot(left, right, precision=lax.Precision.HIGHEST, preferred_element_type=jnp.float32)


def split_table(table):
    upper = lax.optimization_barrier(table.astype(jnp.bfloat16))
    lower = (table - upper.astype(jnp.float32)).astype(jnp.bfloat16)
    return (upper, lower)


def half_matmul(table, signal):
    upper, lower = split_table(table)
    return jnp.dot(upper, signal, preferred_element_type=jnp.float32) + jnp.dot(
        lower, signal, preferred_element_type=jnp.float32
    )


def make_tables(rows):
    index = jnp.arange(rows, dtype=jnp.int32)
    long_index = jnp.arange(2 * rows, dtype=jnp.int32)
    angle = (index[:, None] * index[None, :] % (2 * rows)).astype(jnp.float32) * (math.pi / rows)
    angle_back = (long_index[:, None] * index[None, :] % (2 * rows)).astype(jnp.float32) * (
        math.pi / rows
    )
    weight = jnp.where(index == 0, 1.0, 2.0).astype(jnp.float32) / (2.0 * rows)
    alternate = (1 - 2 * (index % 2)).astype(jnp.float32)
    alternate_back = (1 - 2 * (long_index % 2)).astype(jnp.float32) / (2.0 * rows)
    return (
        jnp.cos(angle),
        -jnp.sin(angle),
        alternate,
        jnp.cos(angle_back) * weight[None, :],
        -jnp.sin(angle_back) * weight[None, :],
        alternate_back,
    )


def forward(signal, tables):
    fwd_cos, fwd_sin, alternate = (tables[0], tables[1], tables[2])
    return (matmul(fwd_cos, signal), matmul(fwd_sin, signal), matmul(alternate[None, :], signal))


def forward_half(signal, tables):
    fwd_cos, fwd_sin, alternate = (tables[0], tables[1], tables[2])
    signs = alternate[None, :].astype(jnp.bfloat16)
    return (
        half_matmul(fwd_cos, signal),
        half_matmul(fwd_sin, signal),
        jnp.dot(signs, signal, preferred_element_type=jnp.float32),
    )


def inverse(spectrum, tables, count):
    inv_cos, inv_sin, alternate_back = (tables[3], tables[4], tables[5])
    return (
        matmul(inv_cos[:count], spectrum[0])
        + matmul(inv_sin[:count], spectrum[1])
        + alternate_back[:count, None] * spectrum[2]
    )


def correlate(first, second):
    real_part = first[0] * second[0] + first[1] * second[1]
    imag_part = first[0] * second[1] - first[1] * second[0]
    return (real_part, imag_part, first[2] * second[2])


def add_lags(filter_terms, lagged, step, active, rows):
    later = jnp.asarray(step >= 1, jnp.float32)
    filter_terms = filter_terms.at[step].add(lagged[:rows] * active)
    return filter_terms.at[jnp.maximum(step - 1, 0)].add(lagged[rows:] * (active * later))


def body(q_proj, k_proj, v_proj, saved_conv, out_grad, out_weight, filter_taps):
    rows = q_proj.shape[0]
    chans = q_proj.shape[1]
    blocks = lax.axis_size("ctx")
    me_index = lax.axis_index("ctx")
    tables = make_tables(rows)
    empty = jnp.zeros((rows, chans), jnp.float32)
    d_gated = lax.dot_general(
        lax.all_gather(out_grad, "tp", axis=1, tiled=True),
        out_weight,
        (((1,), (1,)), ((), ())),
        preferred_element_type=jnp.float32,
    )
    dq_grad = (d_gated * saved_conv.astype(jnp.float32)).astype(jnp.bfloat16)
    dz_local = d_gated * q_proj.astype(jnp.float32)
    gated = (k_proj.astype(jnp.float32) * v_proj.astype(jnp.float32)).astype(jnp.bfloat16)
    whole_filter = lax.all_gather(filter_taps, "ctx", axis=0, tiled=True)
    filter_blocks = whole_filter.reshape(blocks, rows, chans)
    cos_upper, cos_lower = split_table(tables[0])
    sin_upper, sin_lower = split_table(tables[1])
    spec_real = jnp.einsum(
        "fn,bnc->bfc", cos_upper, filter_blocks, preferred_element_type=jnp.float32
    ) + jnp.einsum("fn,bnc->bfc", cos_lower, filter_blocks, preferred_element_type=jnp.float32)
    spec_imag = jnp.einsum(
        "fn,bnc->bfc", sin_upper, filter_blocks, preferred_element_type=jnp.float32
    ) + jnp.einsum("fn,bnc->bfc", sin_lower, filter_blocks, preferred_element_type=jnp.float32)
    spec_top = jnp.einsum(
        "n,bnc->bc",
        tables[2].astype(jnp.bfloat16),
        filter_blocks,
        preferred_element_type=jnp.float32,
    )[:, None, :]
    parity = tables[2][:, None]

    def lag_spectrum(step):
        earlier = jnp.maximum(step - 1, 0)
        keep = jnp.asarray(step >= 1, jnp.float32)
        pieces = []
        for stack, factor in ((spec_real, parity), (spec_imag, parity), (spec_top, 1.0)):
            current = lax.dynamic_index_in_dim(stack, step, 0, keepdims=False)
            before = lax.dynamic_index_in_dim(stack, earlier, 0, keepdims=False)
            pieces.append(current + keep * factor * before)
        return (pieces[0], pieces[1], pieces[2])

    filter_terms = jnp.zeros((blocks, rows, chans), jnp.float32)
    dz_spec = forward(dz_local, tables)

    def carried_step(step, state):
        partial_value, moving, terms = state
        active = jnp.asarray(me_index >= step, jnp.float32)
        partial_value = partial_value + active * inverse(
            correlate(lag_spectrum(step), dz_spec), tables, rows
        )
        moving_spec = forward_half(moving, tables)
        lagged = inverse(correlate(moving_spec, dz_spec), tables, 2 * rows)
        terms = add_lags(terms, lagged, step, active, rows)
        partial_value = from_behind(partial_value, "ctx", 1)
        moving = passed_along(moving, "ctx", 1)
        return (partial_value, moving, terms)

    du_local, moving_last, filter_terms = lax.fori_loop(
        0, blocks, carried_step, (empty, gated, filter_terms)
    )
    summed = lax.psum_scatter(
        filter_terms.reshape(blocks * rows, chans), "ctx", scatter_dimension=0, tiled=True
    )
    filter_grad = summed * float(rows * blocks) ** (-0.5)
    dk_grad = (du_local * v_proj.astype(jnp.float32)).astype(jnp.bfloat16)
    dv_grad = (du_local * k_proj.astype(jnp.float32)).astype(jnp.bfloat16)
    return (dq_grad, dk_grad, dv_grad, filter_grad)


def solution(mesh):
    in_specs = (
        P("ctx", "tp"),
        P("ctx", "tp"),
        P("ctx", "tp"),
        P("ctx", "tp"),
        P("ctx", "tp"),
        P("tp", None),
        P("ctx", "tp"),
    )
    out_specs = (P("ctx", "tp"), P("ctx", "tp"), P("ctx", "tp"), P("ctx", "tp"))
    return jax.shard_map(body, mesh=mesh, in_specs=in_specs, out_specs=out_specs, check_vma=False)
```

profile of v0, /device:TPU:2, one launch (start us, length us, event | category | flops | bytes accessed | tf_op | source)
XLA Modules:
  0.0 925.3 jit_solution(6137578330895444131)
XLA Ops:
  10.7 76.7 %all-gather.3.cloned.1.call-done = bf16[128,4096]{1,0:T(8,128)(2,1)} async-done(((bf16[128,256]{1,0:T(8,128)(2,1)}), bf16[128,4096]{1,0:T(8,128)(2,1)}) %all-gather.3.cloned.1.call-update) | async-done | bytes 1048592 | tf_op jit(solution)/shard_map/all_gather | solution.py:101
  87.5 2.7 multiply_convert_fusion
  92.2 89.1 %all-gather.5.cloned.1.call-done = bf16[4096,256]{1,0:T(8,128)(2,1)} async-done(((bf16[128,256]{1,0:T(8,128)(2,1)}), bf16[4096,256]{1,0:T(8,128)(2,1)}) %all-gather.5.cloned.1.call-update) | async-done | bytes 2097168 | tf_op jit(solution)/shard_map/all_gather | solution.py:109
  183.5 2.3 fusion.106
  185.8 2.9 add_bitcast_fusion
  189.4 2.9 add_bitcast_fusion.1
  192.3 2.5 broadcast_in_dim.41
  194.8 567.6 %while.23 = (s32[]{:T(128)}, f32[128,256]{0,1:T(8,128)S(1)}, bf16[128,256]{1,0:T(8,128)(2,1)S(1)}, f32[32,128,256]{1,2,0:T(8,128)}, s32[]{:T(128)}, /*index=5*/f...) while((s32[]{:T(128)}, f32[128,256]{0,1:T(8,128)S(1)}, ...), condition=%wide.region_3.4_spmd.clone.clone, body=%wide.region_0.3_spmd.clone.clone.sunk | while | flops 337464864 | bytes 7294348 | solution.py:153
  209.6 2.9 collective-permute-done
  217.2 5.4 collective-permute-start
  235.3 3.9 collective-permute-start
  241.9 2.3 fusion.230
  252.2 5.7 collective-permute-start
  260.6 2.3 fusion.230
  270.6 3.9 collective-permute-start
  277.3 2.3 fusion.230
  287.5 6.9 collective-permute-start
  297.2 2.3 fusion.230
  307.2 3.9 collective-permute-start
  313.8 2.3 fusion.230
  324.1 5.4 collective-permute-start
  332.3 2.3 fusion.230
  342.2 5.1 collective-permute-start
  359.8 5.4 collective-permute-start
  367.9 2.3 fusion.230
  377.9 5.1 collective-permute-start
  385.7 2.3 fusion.230
  395.4 5.1 collective-permute-start
  413.2 5.0 collective-permute-start
  430.8 5.0 collective-permute-start
  438.6 2.3 fusion.230
  448.4 5.0 collective-permute-start
  456.3 2.3 fusion.230
  466.0 5.1 collective-permute-start
  473.8 2.3 fusion.230
  478.3 2.8 collective-permute-start.1
  484.4 5.1 collective-permute-start
  492.2 2.3 fusion.230
  501.9 5.1 collective-permute-start
  509.7 2.3 fusion.230
  519.4 5.0 collective-permute-start
  537.0 5.1 collective-permute-start
  544.8 2.3 fusion.230
  554.8 5.1 collective-permute-start
  562.6 2.3 fusion.230
  572.3 5.1 collective-permute-start
  584.6 3.3 collective-permute-start.1
  591.3 5.0 collective-permute-start
  608.8 5.1 collective-permute-start
  616.6 2.3 fusion.230
  626.3 5.1 collective-permute-start
  643.9 5.1 collective-permute-start
  651.7 2.3 fusion.230
  656.2 2.5 collective-permute-start.1
  661.9 5.0 collective-permute-start
  679.5 5.1 collective-permute-start
  697.3 5.0 collective-permute-start
  714.8 5.1 collective-permute-start
  722.6 2.3 fusion.230
  732.5 5.1 collective-permute-start
  740.4 2.3 fusion.230
  750.1 5.1 collective-permute-start
  762.4 5.6 copy.13
  769.6 147.7 %reduce-scatter.2.cloned.1.call-done = f32[128,256]{1,0:T(8,128)} async-done(((f32[4096,256]{1,0:T(8,128)}), f32[128,256]{1,0:T(8,128)}) %reduce-scatter.2.cloned.1.call-update) | async-done | bytes 131088 | tf_op jit(solution)/shard_map/reduce_scatter | solution.py:156
  (653 shorter events, 364.7 us)
Async XLA Ops:
  7.2 80.3 %all-gather.3.cloned.1.call-start = ((), (), s32[]{:S(2)}) async-start(), calls=%async_computation.1 | async-start | bytes 1114112 | tf_op jit(solution)/shard_map/all_gather | solution.py:101
  7.9 173.4 %all-gather.5.cloned.1.call-start = ((), (), s32[]{:S(2)}) async-start(), calls=%async_computation.2 | async-start | bytes 2162688 | tf_op jit(solution)/shard_map/all_gather | solution.py:109
  8.7 908.6 %reduce-scatter.2.cloned.1.call-start = ((), (), s32[]{:S(2)}) async-start(), calls=%async_computation.3 | async-start | bytes 4325376 | tf_op jit(solution)/shard_map/reduce_scatter | solution.py:156
  194.8 14.8 %collective-permute-start.1 = (bf16[128,256]{1,0:T(8,128)(2,1)S(1)}, bf16[128,256]{1,0:T(8,128)(2,1)S(1)}, u32[]{:S(2)}, u32[]{:S(2)}) collective-permute-start(bf16[128,256]{1,0:T(8,128)(2,1)S(1)} %copy.25), channel_id=1, source_target_pairs={{0,16},{16,32},{32,48},{48,64},{64,80},{80,96},{96,112},{112,128},... | collective-permute-start | bytes 196616 | tf_op jit(solution)/shard_map/while/body/eval_jaxpr/ppermute | solution.py:17
  200.3 12.3 %collective-permute-start = (f32[128,256]{0,1:T(8,128)S(1)}, f32[128,256]{0,1:T(8,128)S(1)}, u32[]{:S(2)}, u32[]{:S(2)}) collective-permute-start(f32[128,256]{0,1:T(8,128)S(1)} %fusion.225), channel_id=1, source_target_pairs={{0,16},{16,32},{32,48},{48,64},{64,80},{80,96},{96,112},{112,128},... | collective-permute-start | bytes 393224 | tf_op jit(solution)/shard_map/while/body/eval_jaxpr/ppermute | solution.py:11
  212.6 17.2 %collective-permute-start.1 = (bf16[128,256]{1,0:T(8,128)(2,1)S(1)}, bf16[128,256]{1,0:T(8,128)(2,1)S(1)}, u32[]{:S(2)}, u32[]{:S(2)}) collective-permute-start(bf16[128,256]{1,0:T(8,128)(2,1)S(1)} %copy.25), channel_id=1, source_target_pairs={{0,16},{16,32},{32,48},{48,64},{64,80},{80,96},{96,112},{112,128},... | collective-permute-start | bytes 196616 | tf_op jit(solution)/shard_map/while/body/eval_jaxpr/ppermute | solution.py:17
  217.2 12.6 %collective-permute-start = (f32[128,256]{0,1:T(8,128)S(1)}, f32[128,256]{0,1:T(8,128)S(1)}, u32[]{:S(2)}, u32[]{:S(2)}) collective-permute-start(f32[128,256]{0,1:T(8,128)S(1)} %fusion.225), channel_id=1, source_target_pairs={{0,16},{16,32},{32,48},{48,64},{64,80},{80,96},{96,112},{112,128},... | collective-permute-start | bytes 393224 | tf_op jit(solution)/shard_map/while/body/eval_jaxpr/ppermute | solution.py:11
  229.7 16.6 %collective-permute-start.1 = (bf16[128,256]{1,0:T(8,128)(2,1)S(1)}, bf16[128,256]{1,0:T(8,128)(2,1)S(1)}, u32[]{:S(2)}, u32[]{:S(2)}) collective-permute-start(bf16[128,256]{1,0:T(8,128)(2,1)S(1)} %copy.25), channel_id=1, source_target_pairs={{0,16},{16,32},{32,48},{48,64},{64,80},{80,96},{96,112},{112,128},... | collective-permute-start | bytes 196616 | tf_op jit(solution)/shard_map/while/body/eval_jaxpr/ppermute | solution.py:17
  235.3 12.3 %collective-permute-start = (f32[128,256]{0,1:T(8,128)S(1)}, f32[128,256]{0,1:T(8,128)S(1)}, u32[]{:S(2)}, u32[]{:S(2)}) collective-permute-start(f32[128,256]{0,1:T(8,128)S(1)} %fusion.225), channel_id=1, source_target_pairs={{0,16},{16,32},{32,48},{48,64},{64,80},{80,96},{96,112},{112,128},... | collective-permute-start | bytes 393224 | tf_op jit(solution)/shard_map/while/body/eval_jaxpr/ppermute | solution.py:11
  247.6 17.6 %collective-permute-start.1 = (bf16[128,256]{1,0:T(8,128)(2,1)S(1)}, bf16[128,256]{1,0:T(8,128)(2,1)S(1)}, u32[]{:S(2)}, u32[]{:S(2)}) collective-permute-start(bf16[128,256]{1,0:T(8,128)(2,1)S(1)} %copy.25), channel_id=1, source_target_pairs={{0,16},{16,32},{32,48},{48,64},{64,80},{80,96},{96,112},{112,128},... | collective-permute-start | bytes 196616 | tf_op jit(solution)/shard_map/while/body/eval_jaxpr/ppermute | solution.py:17
  252.2 13.0 %collective-permute-start = (f32[128,256]{0,1:T(8,128)S(1)}, f32[128,256]{0,1:T(8,128)S(1)}, u32[]{:S(2)}, u32[]{:S(2)}) collective-permute-start(f32[128,256]{0,1:T(8,128)S(1)} %fusion.225), channel_id=1, source_target_pairs={{0,16},{16,32},{32,48},{48,64},{64,80},{80,96},{96,112},{112,128},... | collective-permute-start | bytes 393224 | tf_op jit(solution)/shard_map/while/body/eval_jaxpr/ppermute | solution.py:11
  265.1 16.6 %collective-permute-start.1 = (bf16[128,256]{1,0:T(8,128)(2,1)S(1)}, bf16[128,256]{1,0:T(8,128)(2,1)S(1)}, u32[]{:S(2)}, u32[]{:S(2)}) collective-permute-start(bf16[128,256]{1,0:T(8,128)(2,1)S(1)} %copy.25), channel_id=1, source_target_pairs={{0,16},{16,32},{32,48},{48,64},{64,80},{80,96},{96,112},{112,128},... | collective-permute-start | bytes 196616 | tf_op jit(solution)/shard_map/while/body/eval_jaxpr/ppermute | solution.py:17
  270.6 12.3 %collective-permute-start = (f32[128,256]{0,1:T(8,128)S(1)}, f32[128,256]{0,1:T(8,128)S(1)}, u32[]{:S(2)}, u32[]{:S(2)}) collective-permute-start(f32[128,256]{0,1:T(8,128)S(1)} %fusion.225), channel_id=1, source_target_pairs={{0,16},{16,32},{32,48},{48,64},{64,80},{80,96},{96,112},{112,128},... | collective-permute-start | bytes 393224 | tf_op jit(solution)/shard_map/while/body/eval_jaxpr/ppermute | solution.py:11
  282.9 18.7 %collective-permute-start.1 = (bf16[128,256]{1,0:T(8,128)(2,1)S(1)}, bf16[128,256]{1,0:T(8,128)(2,1)S(1)}, u32[]{:S(2)}, u32[]{:S(2)}) collective-permute-start(bf16[128,256]{1,0:T(8,128)(2,1)S(1)} %copy.25), channel_id=1, source_target_pairs={{0,16},{16,32},{32,48},{48,64},{64,80},{80,96},{96,112},{112,128},... | collective-permute-start | bytes 196616 | tf_op jit(solution)/shard_map/while/body/eval_jaxpr/ppermute | solution.py:17
  287.5 14.1 %collective-permute-start = (f32[128,256]{0,1:T(8,128)S(1)}, f32[128,256]{0,1:T(8,128)S(1)}, u32[]{:S(2)}, u32[]{:S(2)}) collective-permute-start(f32[128,256]{0,1:T(8,128)S(1)} %fusion.225), channel_id=1, source_target_pairs={{0,16},{16,32},{32,48},{48,64},{64,80},{80,96},{96,112},{112,128},... | collective-permute-start | bytes 393224 | tf_op jit(solution)/shard_map/while/body/eval_jaxpr/ppermute | solution.py:11
  301.7 16.6 %collective-permute-start.1 = (bf16[128,256]{1,0:T(8,128)(2,1)S(1)}, bf16[128,256]{1,0:T(8,128)(2,1)S(1)}, u32[]{:S(2)}, u32[]{:S(2)}) collective-permute-start(bf16[128,256]{1,0:T(8,128)(2,1)S(1)} %copy.25), channel_id=1, source_target_pairs={{0,16},{16,32},{32,48},{48,64},{64,80},{80,96},{96,112},{112,128},... | collective-permute-start | bytes 196616 | tf_op jit(solution)/shard_map/while/body/eval_jaxpr/ppermute | solution.py:17
  307.2 12.3 %collective-permute-start = (f32[128,256]{0,1:T(8,128)S(1)}, f32[128,256]{0,1:T(8,128)S(1)}, u32[]{:S(2)}, u32[]{:S(2)}) collective-permute-start(f32[128,256]{0,1:T(8,128)S(1)} %fusion.225), channel_id=1, source_target_pairs={{0,16},{16,32},{32,48},{48,64},{64,80},{80,96},{96,112},{112,128},... | collective-permute-start | bytes 393224 | tf_op jit(solution)/shard_map/while/body/eval_jaxpr/ppermute | solution.py:11
  319.5 17.3 %collective-permute-start.1 = (bf16[128,256]{1,0:T(8,128)(2,1)S(1)}, bf16[128,256]{1,0:T(8,128)(2,1)S(1)}, u32[]{:S(2)}, u32[]{:S(2)}) collective-permute-start(bf16[128,256]{1,0:T(8,128)(2,1)S(1)} %copy.25), channel_id=1, source_target_pairs={{0,16},{16,32},{32,48},{48,64},{64,80},{80,96},{96,112},{112,128},... | collective-permute-start | bytes 196616 | tf_op jit(solution)/shard_map/while/body/eval_jaxpr/ppermute | solution.py:17
  324.1 12.7 %collective-permute-start = (f32[128,256]{0,1:T(8,128)S(1)}, f32[128,256]{0,1:T(8,128)S(1)}, u32[]{:S(2)}, u32[]{:S(2)}) collective-permute-start(f32[128,256]{0,1:T(8,128)S(1)} %fusion.225), channel_id=1, source_target_pairs={{0,16},{16,32},{32,48},{48,64},{64,80},{80,96},{96,112},{112,128},... | collective-permute-start | bytes 393224 | tf_op jit(solution)/shard_map/while/body/eval_jaxpr/ppermute | solution.py:11
  336.7 17.8 %collective-permute-start.1 = (bf16[128,256]{1,0:T(8,128)(2,1)S(1)}, bf16[128,256]{1,0:T(8,128)(2,1)S(1)}, u32[]{:S(2)}, u32[]{:S(2)}) collective-permute-start(bf16[128,256]{1,0:T(8,128)(2,1)S(1)} %copy.25), channel_id=1, source_target_pairs={{0,16},{16,32},{32,48},{48,64},{64,80},{80,96},{96,112},{112,128},... | collective-permute-start | bytes 196616 | tf_op jit(solution)/shard_map/while/body/eval_jaxpr/ppermute | solution.py:17
  342.2 12.3 %collective-permute-start = (f32[128,256]{0,1:T(8,128)S(1)}, f32[128,256]{0,1:T(8,128)S(1)}, u32[]{:S(2)}, u32[]{:S(2)}) collective-permute-start(f32[128,256]{0,1:T(8,128)S(1)} %fusion.225), channel_id=1, source_target_pairs={{0,16},{16,32},{32,48},{48,64},{64,80},{80,96},{96,112},{112,128},... | collective-permute-start | bytes 393224 | tf_op jit(solution)/shard_map/while/body/eval_jaxpr/ppermute | solution.py:11
  354.6 17.8 %collective-permute-start.1 = (bf16[128,256]{1,0:T(8,128)(2,1)S(1)}, bf16[128,256]{1,0:T(8,128)(2,1)S(1)}, u32[]{:S(2)}, u32[]{:S(2)}) collective-permute-start(bf16[128,256]{1,0:T(8,128)(2,1)S(1)} %copy.25), channel_id=1, source_target_pairs={{0,16},{16,32},{32,48},{48,64},{64,80},{80,96},{96,112},{112,128},... | collective-permute-start | bytes 196616 | tf_op jit(solution)/shard_map/while/body/eval_jaxpr/ppermute | solution.py:17
  359.8 12.6 %collective-permute-start = (f32[128,256]{0,1:T(8,128)S(1)}, f32[128,256]{0,1:T(8,128)S(1)}, u32[]{:S(2)}, u32[]{:S(2)}) collective-permute-start(f32[128,256]{0,1:T(8,128)S(1)} %fusion.225), channel_id=1, source_target_pairs={{0,16},{16,32},{32,48},{48,64},{64,80},{80,96},{96,112},{112,128},... | collective-permute-start | bytes 393224 | tf_op jit(solution)/shard_map/while/body/eval_jaxpr/ppermute | solution.py:11
  372.4 17.8 %collective-permute-start.1 = (bf16[128,256]{1,0:T(8,128)(2,1)S(1)}, bf16[128,256]{1,0:T(8,128)(2,1)S(1)}, u32[]{:S(2)}, u32[]{:S(2)}) collective-permute-start(bf16[128,256]{1,0:T(8,128)(2,1)S(1)} %copy.25), channel_id=1, source_target_pairs={{0,16},{16,32},{32,48},{48,64},{64,80},{80,96},{96,112},{112,128},... | collective-permute-start | bytes 196616 | tf_op jit(solution)/shard_map/while/body/eval_jaxpr/ppermute | solution.py:17
  377.9 12.3 %collective-permute-start = (f32[128,256]{0,1:T(8,128)S(1)}, f32[128,256]{0,1:T(8,128)S(1)}, u32[]{:S(2)}, u32[]{:S(2)}) collective-permute-start(f32[128,256]{0,1:T(8,128)S(1)} %fusion.225), channel_id=1, source_target_pairs={{0,16},{16,32},{32,48},{48,64},{64,80},{80,96},{96,112},{112,128},... | collective-permute-start | bytes 393224 | tf_op jit(solution)/shard_map/while/body/eval_jaxpr/ppermute | solution.py:11
  390.2 17.6 %collective-permute-start.1 = (bf16[128,256]{1,0:T(8,128)(2,1)S(1)}, bf16[128,256]{1,0:T(8,128)(2,1)S(1)}, u32[]{:S(2)}, u32[]{:S(2)}) collective-permute-start(bf16[128,256]{1,0:T(8,128)(2,1)S(1)} %copy.25), channel_id=1, source_target_pairs={{0,16},{16,32},{32,48},{48,64},{64,80},{80,96},{96,112},{112,128},... | collective-permute-start | bytes 196616 | tf_op jit(solution)/shard_map/while/body/eval_jaxpr/ppermute | solution.py:17
  395.4 12.3 %collective-permute-start = (f32[128,256]{0,1:T(8,128)S(1)}, f32[128,256]{0,1:T(8,128)S(1)}, u32[]{:S(2)}, u32[]{:S(2)}) collective-permute-start(f32[128,256]{0,1:T(8,128)S(1)} %fusion.225), channel_id=1, source_target_pairs={{0,16},{16,32},{32,48},{48,64},{64,80},{80,96},{96,112},{112,128},... | collective-permute-start | bytes 393224 | tf_op jit(solution)/shard_map/while/body/eval_jaxpr/ppermute | solution.py:11
  407.8 17.7 %collective-permute-start.1 = (bf16[128,256]{1,0:T(8,128)(2,1)S(1)}, bf16[128,256]{1,0:T(8,128)(2,1)S(1)}, u32[]{:S(2)}, u32[]{:S(2)}) collective-permute-start(bf16[128,256]{1,0:T(8,128)(2,1)S(1)} %copy.25), channel_id=1, source_target_pairs={{0,16},{16,32},{32,48},{48,64},{64,80},{80,96},{96,112},{112,128},... | collective-permute-start | bytes 196616 | tf_op jit(solution)/shard_map/while/body/eval_jaxpr/ppermute | solution.py:17
  413.2 12.3 %collective-permute-start = (f32[128,256]{0,1:T(8,128)S(1)}, f32[128,256]{0,1:T(8,128)S(1)}, u32[]{:S(2)}, u32[]{:S(2)}) collective-permute-start(f32[128,256]{0,1:T(8,128)S(1)} %fusion.225), channel_id=1, source_target_pairs={{0,16},{16,32},{32,48},{48,64},{64,80},{80,96},{96,112},{112,128},... | collective-permute-start | bytes 393224 | tf_op jit(solution)/shard_map/while/body/eval_jaxpr/ppermute | solution.py:11
  425.6 17.5 %collective-permute-start.1 = (bf16[128,256]{1,0:T(8,128)(2,1)S(1)}, bf16[128,256]{1,0:T(8,128)(2,1)S(1)}, u32[]{:S(2)}, u32[]{:S(2)}) collective-permute-start(bf16[128,256]{1,0:T(8,128)(2,1)S(1)} %copy.25), channel_id=1, source_target_pairs={{0,16},{16,32},{32,48},{48,64},{64,80},{80,96},{96,112},{112,128},... | collective-permute-start | bytes 196616 | tf_op jit(solution)/shard_map/while/body/eval_jaxpr/ppermute | solution.py:17
  430.8 12.3 %collective-permute-start = (f32[128,256]{0,1:T(8,128)S(1)}, f32[128,256]{0,1:T(8,128)S(1)}, u32[]{:S(2)}, u32[]{:S(2)}) collective-permute-start(f32[128,256]{0,1:T(8,128)S(1)} %fusion.225), channel_id=1, source_target_pairs={{0,16},{16,32},{32,48},{48,64},{64,80},{80,96},{96,112},{112,128},... | collective-permute-start | bytes 393224 | tf_op jit(solution)/shard_map/while/body/eval_jaxpr/ppermute | solution.py:11
  443.1 17.7 %collective-permute-start.1 = (bf16[128,256]{1,0:T(8,128)(2,1)S(1)}, bf16[128,256]{1,0:T(8,128)(2,1)S(1)}, u32[]{:S(2)}, u32[]{:S(2)}) collective-permute-start(bf16[128,256]{1,0:T(8,128)(2,1)S(1)} %copy.25), channel_id=1, source_target_pairs={{0,16},{16,32},{32,48},{48,64},{64,80},{80,96},{96,112},{112,128},... | collective-permute-start | bytes 196616 | tf_op jit(solution)/shard_map/while/body/eval_jaxpr/ppermute | solution.py:17
  448.4 12.3 %collective-permute-start = (f32[128,256]{0,1:T(8,128)S(1)}, f32[128,256]{0,1:T(8,128)S(1)}, u32[]{:S(2)}, u32[]{:S(2)}) collective-permute-start(f32[128,256]{0,1:T(8,128)S(1)} %fusion.225), channel_id=1, source_target_pairs={{0,16},{16,32},{32,48},{48,64},{64,80},{80,96},{96,112},{112,128},... | collective-permute-start | bytes 393224 | tf_op jit(solution)/shard_map/while/body/eval_jaxpr/ppermute | solution.py:11
  460.8 17.5 %collective-permute-start.1 = (bf16[128,256]{1,0:T(8,128)(2,1)S(1)}, bf16[128,256]{1,0:T(8,128)(2,1)S(1)}, u32[]{:S(2)}, u32[]{:S(2)}) collective-permute-start(bf16[128,256]{1,0:T(8,128)(2,1)S(1)} %copy.25), channel_id=1, source_target_pairs={{0,16},{16,32},{32,48},{48,64},{64,80},{80,96},{96,112},{112,128},... | collective-permute-start | bytes 196616 | tf_op jit(solution)/shard_map/while/body/eval_jaxpr/ppermute | solution.py:17
  466.0 12.3 %collective-permute-start = (f32[128,256]{0,1:T(8,128)S(1)}, f32[128,256]{0,1:T(8,128)S(1)}, u32[]{:S(2)}, u32[]{:S(2)}) collective-permute-start(f32[128,256]{0,1:T(8,128)S(1)} %fusion.225), channel_id=1, source_target_pairs={{0,16},{16,32},{32,48},{48,64},{64,80},{80,96},{96,112},{112,128},... | collective-permute-start | bytes 393224 | tf_op jit(solution)/shard_map/while/body/eval_jaxpr/ppermute | solution.py:11
  478.3 18.4 %collective-permute-start.1 = (bf16[128,256]{1,0:T(8,128)(2,1)S(1)}, bf16[128,256]{1,0:T(8,128)(2,1)S(1)}, u32[]{:S(2)}, u32[]{:S(2)}) collective-permute-start(bf16[128,256]{1,0:T(8,128)(2,1)S(1)} %copy.25), channel_id=1, source_target_pairs={{0,16},{16,32},{32,48},{48,64},{64,80},{80,96},{96,112},{112,128},... | collective-permute-start | bytes 196616 | tf_op jit(solution)/shard_map/while/body/eval_jaxpr/ppermute | solution.py:17
  484.4 12.3 %collective-permute-start = (f32[128,256]{0,1:T(8,128)S(1)}, f32[128,256]{0,1:T(8,128)S(1)}, u32[]{:S(2)}, u32[]{:S(2)}) collective-permute-start(f32[128,256]{0,1:T(8,128)S(1)} %fusion.225), channel_id=1, source_target_pairs={{0,16},{16,32},{32,48},{48,64},{64,80},{80,96},{96,112},{112,128},... | collective-permute-start | bytes 393224 | tf_op jit(solution)/shard_map/while/body/eval_jaxpr/ppermute | solution.py:11
  496.7 17.5 %collective-permute-start.1 = (bf16[128,256]{1,0:T(8,128)(2,1)S(1)}, bf16[128,256]{1,0:T(8,128)(2,1)S(1)}, u32[]{:S(2)}, u32[]{:S(2)}) collective-permute-start(bf16[128,256]{1,0:T(8,128)(2,1)S(1)} %copy.25), channel_id=1, source_target_pairs={{0,16},{16,32},{32,48},{48,64},{64,80},{80,96},{96,112},{112,128},... | collective-permute-start | bytes 196616 | tf_op jit(solution)/shard_map/while/body/eval_jaxpr/ppermute | solution.py:17
  501.9 12.3 %collective-permute-start = (f32[128,256]{0,1:T(8,128)S(1)}, f32[128,256]{0,1:T(8,128)S(1)}, u32[]{:S(2)}, u32[]{:S(2)}) collective-permute-start(f32[128,256]{0,1:T(8,128)S(1)} %fusion.225), channel_id=1, source_target_pairs={{0,16},{16,32},{32,48},{48,64},{64,80},{80,96},{96,112},{112,128},... | collective-permute-start | bytes 393224 | tf_op jit(solution)/shard_map/while/body/eval_jaxpr/ppermute | solution.py:11
  514.2 17.5 %collective-permute-start.1 = (bf16[128,256]{1,0:T(8,128)(2,1)S(1)}, bf16[128,256]{1,0:T(8,128)(2,1)S(1)}, u32[]{:S(2)}, u32[]{:S(2)}) collective-permute-start(bf16[128,256]{1,0:T(8,128)(2,1)S(1)} %copy.25), channel_id=1, source_target_pairs={{0,16},{16,32},{32,48},{48,64},{64,80},{80,96},{96,112},{112,128},... | collective-permute-start | bytes 196616 | tf_op jit(solution)/shard_map/while/body/eval_jaxpr/ppermute | solution.py:17
  519.4 12.3 %collective-permute-start = (f32[128,256]{0,1:T(8,128)S(1)}, f32[128,256]{0,1:T(8,128)S(1)}, u32[]{:S(2)}, u32[]{:S(2)}) collective-permute-start(f32[128,256]{0,1:T(8,128)S(1)} %fusion.225), channel_id=1, source_target_pairs={{0,16},{16,32},{32,48},{48,64},{64,80},{80,96},{96,112},{112,128},... | collective-permute-start | bytes 393224 | tf_op jit(solution)/shard_map/while/body/eval_jaxpr/ppermute | solution.py:11
  531.8 17.5 %collective-permute-start.1 = (bf16[128,256]{1,0:T(8,128)(2,1)S(1)}, bf16[128,256]{1,0:T(8,128)(2,1)S(1)}, u32[]{:S(2)}, u32[]{:S(2)}) collective-permute-start(bf16[128,256]{1,0:T(8,128)(2,1)S(1)} %copy.25), channel_id=1, source_target_pairs={{0,16},{16,32},{32,48},{48,64},{64,80},{80,96},{96,112},{112,128},... | collective-permute-start | bytes 196616 | tf_op jit(solution)/shard_map/while/body/eval_jaxpr/ppermute | solution.py:17
  537.0 12.3 %collective-permute-start = (f32[128,256]{0,1:T(8,128)S(1)}, f32[128,256]{0,1:T(8,128)S(1)}, u32[]{:S(2)}, u32[]{:S(2)}) collective-permute-start(f32[128,256]{0,1:T(8,128)S(1)} %fusion.225), channel_id=1, source_target_pairs={{0,16},{16,32},{32,48},{48,64},{64,80},{80,96},{96,112},{112,128},... | collective-permute-start | bytes 393224 | tf_op jit(solution)/shard_map/while/body/eval_jaxpr/ppermute | solution.py:11
  549.3 17.8 %collective-permute-start.1 = (bf16[128,256]{1,0:T(8,128)(2,1)S(1)}, bf16[128,256]{1,0:T(8,128)(2,1)S(1)}, u32[]{:S(2)}, u32[]{:S(2)}) collective-permute-start(bf16[128,256]{1,0:T(8,128)(2,1)S(1)} %copy.25), channel_id=1, source_target_pairs={{0,16},{16,32},{32,48},{48,64},{64,80},{80,96},{96,112},{112,128},... | collective-permute-start | bytes 196616 | tf_op jit(solution)/shard_map/while/body/eval_jaxpr/ppermute | solution.py:17
  554.8 12.3 %collective-permute-start = (f32[128,256]{0,1:T(8,128)S(1)}, f32[128,256]{0,1:T(8,128)S(1)}, u32[]{:S(2)}, u32[]{:S(2)}) collective-permute-start(f32[128,256]{0,1:T(8,128)S(1)} %fusion.225), channel_id=1, source_target_pairs={{0,16},{16,32},{32,48},{48,64},{64,80},{80,96},{96,112},{112,128},... | collective-permute-start | bytes 393224 | tf_op jit(solution)/shard_map/while/body/eval_jaxpr/ppermute | solution.py:11
  567.1 17.5 %collective-permute-start.1 = (bf16[128,256]{1,0:T(8,128)(2,1)S(1)}, bf16[128,256]{1,0:T(8,128)(2,1)S(1)}, u32[]{:S(2)}, u32[]{:S(2)}) collective-permute-start(bf16[128,256]{1,0:T(8,128)(2,1)S(1)} %copy.25), channel_id=1, source_target_pairs={{0,16},{16,32},{32,48},{48,64},{64,80},{80,96},{96,112},{112,128},... | collective-permute-start | bytes 196616 | tf_op jit(solution)/shard_map/while/body/eval_jaxpr/ppermute | solution.py:17
  572.3 12.3 %collective-permute-start = (f32[128,256]{0,1:T(8,128)S(1)}, f32[128,256]{0,1:T(8,128)S(1)}, u32[]{:S(2)}, u32[]{:S(2)}) collective-permute-start(f32[128,256]{0,1:T(8,128)S(1)} %fusion.225), channel_id=1, source_target_pairs={{0,16},{16,32},{32,48},{48,64},{64,80},{80,96},{96,112},{112,128},... | collective-permute-start | bytes 393224 | tf_op jit(solution)/shard_map/while/body/eval_jaxpr/ppermute | solution.py:11
  584.6 18.9 %collective-permute-start.1 = (bf16[128,256]{1,0:T(8,128)(2,1)S(1)}, bf16[128,256]{1,0:T(8,128)(2,1)S(1)}, u32[]{:S(2)}, u32[]{:S(2)}) collective-permute-start(bf16[128,256]{1,0:T(8,128)(2,1)S(1)} %copy.25), channel_id=1, source_target_pairs={{0,16},{16,32},{32,48},{48,64},{64,80},{80,96},{96,112},{112,128},... | collective-permute-start | bytes 196616 | tf_op jit(solution)/shard_map/while/body/eval_jaxpr/ppermute | solution.py:17
  591.3 12.3 %collective-permute-start = (f32[128,256]{0,1:T(8,128)S(1)}, f32[128,256]{0,1:T(8,128)S(1)}, u32[]{:S(2)}, u32[]{:S(2)}) collective-permute-start(f32[128,256]{0,1:T(8,128)S(1)} %fusion.225), channel_id=1, source_target_pairs={{0,16},{16,32},{32,48},{48,64},{64,80},{80,96},{96,112},{112,128},... | collective-permute-start | bytes 393224 | tf_op jit(solution)/shard_map/while/body/eval_jaxpr/ppermute | solution.py:11
  603.6 17.5 %collective-permute-start.1 = (bf16[128,256]{1,0:T(8,128)(2,1)S(1)}, bf16[128,256]{1,0:T(8,128)(2,1)S(1)}, u32[]{:S(2)}, u32[]{:S(2)}) collective-permute-start(bf16[128,256]{1,0:T(8,128)(2,1)S(1)} %copy.25), channel_id=1, source_target_pairs={{0,16},{16,32},{32,48},{48,64},{64,80},{80,96},{96,112},{112,128},... | collective-permute-start | bytes 196616 | tf_op jit(solution)/shard_map/while/body/eval_jaxpr/ppermute | solution.py:17
  608.8 12.3 %collective-permute-start = (f32[128,256]{0,1:T(8,128)S(1)}, f32[128,256]{0,1:T(8,128)S(1)}, u32[]{:S(2)}, u32[]{:S(2)}) collective-permute-start(f32[128,256]{0,1:T(8,128)S(1)} %fusion.225), channel_id=1, source_target_pairs={{0,16},{16,32},{32,48},{48,64},{64,80},{80,96},{96,112},{112,128},... | collective-permute-start | bytes 393224 | tf_op jit(solution)/shard_map/while/body/eval_jaxpr/ppermute | solution.py:11
  621.1 17.5 %collective-permute-start.1 = (bf16[128,256]{1,0:T(8,128)(2,1)S(1)}, bf16[128,256]{1,0:T(8,128)(2,1)S(1)}, u32[]{:S(2)}, u32[]{:S(2)}) collective-permute-start(bf16[128,256]{1,0:T(8,128)(2,1)S(1)} %copy.25), channel_id=1, source_target_pairs={{0,16},{16,32},{32,48},{48,64},{64,80},{80,96},{96,112},{112,128},... | collective-permute-start | bytes 196616 | tf_op jit(solution)/shard_map/while/body/eval_jaxpr/ppermute | solution.py:17
  626.3 12.3 %collective-permute-start = (f32[128,256]{0,1:T(8,128)S(1)}, f32[128,256]{0,1:T(8,128)S(1)}, u32[]{:S(2)}, u32[]{:S(2)}) collective-permute-start(f32[128,256]{0,1:T(8,128)S(1)} %fusion.225), channel_id=1, source_target_pairs={{0,16},{16,32},{32,48},{48,64},{64,80},{80,96},{96,112},{112,128},... | collective-permute-start | bytes 393224 | tf_op jit(solution)/shard_map/while/body/eval_jaxpr/ppermute | solution.py:11
  638.6 17.5 %collective-permute-start.1 = (bf16[128,256]{1,0:T(8,128)(2,1)S(1)}, bf16[128,256]{1,0:T(8,128)(2,1)S(1)}, u32[]{:S(2)}, u32[]{:S(2)}) collective-permute-start(bf16[128,256]{1,0:T(8,128)(2,1)S(1)} %copy.25), channel_id=1, source_target_pairs={{0,16},{16,32},{32,48},{48,64},{64,80},{80,96},{96,112},{112,128},... | collective-permute-start | bytes 196616 | tf_op jit(solution)/shard_map/while/body/eval_jaxpr/ppermute | solution.py:17
  643.9 12.3 %collective-permute-start = (f32[128,256]{0,1:T(8,128)S(1)}, f32[128,256]{0,1:T(8,128)S(1)}, u32[]{:S(2)}, u32[]{:S(2)}) collective-permute-start(f32[128,256]{0,1:T(8,128)S(1)} %fusion.225), channel_id=1, source_target_pairs={{0,16},{16,32},{32,48},{48,64},{64,80},{80,96},{96,112},{112,128},... | collective-permute-start | bytes 393224 | tf_op jit(solution)/shard_map/while/body/eval_jaxpr/ppermute | solution.py:11
  656.2 18.0 %collective-permute-start.1 = (bf16[128,256]{1,0:T(8,128)(2,1)S(1)}, bf16[128,256]{1,0:T(8,128)(2,1)S(1)}, u32[]{:S(2)}, u32[]{:S(2)}) collective-permute-start(bf16[128,256]{1,0:T(8,128)(2,1)S(1)} %copy.25), channel_id=1, source_target_pairs={{0,16},{16,32},{32,48},{48,64},{64,80},{80,96},{96,112},{112,128},... | collective-permute-start | bytes 196616 | tf_op jit(solution)/shard_map/while/body/eval_jaxpr/ppermute | solution.py:17
  674.2 17.5 %collective-permute-start.1 = (bf16[128,256]{1,0:T(8,128)(2,1)S(1)}, bf16[128,256]{1,0:T(8,128)(2,1)S(1)}, u32[]{:S(2)}, u32[]{:S(2)}) collective-permute-start(bf16[128,256]{1,0:T(8,128)(2,1)S(1)} %copy.25), channel_id=1, source_target_pairs={{0,16},{16,32},{32,48},{48,64},{64,80},{80,96},{96,112},{112,128},... | collective-permute-start | bytes 196616 | tf_op jit(solution)/shard_map/while/body/eval_jaxpr/ppermute | solution.py:17
  691.8 17.8 %collective-permute-start.1 = (bf16[128,256]{1,0:T(8,128)(2,1)S(1)}, bf16[128,256]{1,0:T(8,128)(2,1)S(1)}, u32[]{:S(2)}, u32[]{:S(2)}) collective-permute-start(bf16[128,256]{1,0:T(8,128)(2,1)S(1)} %copy.25), channel_id=1, source_target_pairs={{0,16},{16,32},{32,48},{48,64},{64,80},{80,96},{96,112},{112,128},... | collective-permute-start | bytes 196616 | tf_op jit(solution)/shard_map/while/body/eval_jaxpr/ppermute | solution.py:17
  709.6 17.5 %collective-permute-start.1 = (bf16[128,256]{1,0:T(8,128)(2,1)S(1)}, bf16[128,256]{1,0:T(8,128)(2,1)S(1)}, u32[]{:S(2)}, u32[]{:S(2)}) collective-permute-start(bf16[128,256]{1,0:T(8,128)(2,1)S(1)} %copy.25), channel_id=1, source_target_pairs={{0,16},{16,32},{32,48},{48,64},{64,80},{80,96},{96,112},{112,128},... | collective-permute-start | bytes 196616 | tf_op jit(solution)/shard_map/while/body/eval_jaxpr/ppermute | solution.py:17
  714.8 12.3 %collective-permute-start = (f32[128,256]{0,1:T(8,128)S(1)}, f32[128,256]{0,1:T(8,128)S(1)}, u32[]{:S(2)}, u32[]{:S(2)}) collective-permute-start(f32[128,256]{0,1:T(8,128)S(1)} %fusion.225), channel_id=1, source_target_pairs={{0,16},{16,32},{32,48},{48,64},{64,80},{80,96},{96,112},{112,128},... | collective-permute-start | bytes 393224 | tf_op jit(solution)/shard_map/while/body/eval_jaxpr/ppermute | solution.py:11
  727.1 17.7 %collective-permute-start.1 = (bf16[128,256]{1,0:T(8,128)(2,1)S(1)}, bf16[128,256]{1,0:T(8,128)(2,1)S(1)}, u32[]{:S(2)}, u32[]{:S(2)}) collective-permute-start(bf16[128,256]{1,0:T(8,128)(2,1)S(1)} %copy.25), channel_id=1, source_target_pairs={{0,16},{16,32},{32,48},{48,64},{64,80},{80,96},{96,112},{112,128},... | collective-permute-start | bytes 196616 | tf_op jit(solution)/shard_map/while/body/eval_jaxpr/ppermute | solution.py:17
  732.5 12.3 %collective-permute-start = (f32[128,256]{0,1:T(8,128)S(1)}, f32[128,256]{0,1:T(8,128)S(1)}, u32[]{:S(2)}, u32[]{:S(2)}) collective-permute-start(f32[128,256]{0,1:T(8,128)S(1)} %fusion.225), channel_id=1, source_target_pairs={{0,16},{16,32},{32,48},{48,64},{64,80},{80,96},{96,112},{112,128},... | collective-permute-start | bytes 393224 | tf_op jit(solution)/shard_map/while/body/eval_jaxpr/ppermute | solution.py:11
  744.9 17.5 %collective-permute-start.1 = (bf16[128,256]{1,0:T(8,128)(2,1)S(1)}, bf16[128,256]{1,0:T(8,128)(2,1)S(1)}, u32[]{:S(2)}, u32[]{:S(2)}) collective-permute-start(bf16[128,256]{1,0:T(8,128)(2,1)S(1)} %copy.25), channel_id=1, source_target_pairs={{0,16},{16,32},{32,48},{48,64},{64,80},{80,96},{96,112},{112,128},... | collective-permute-start | bytes 196616 | tf_op jit(solution)/shard_map/while/body/eval_jaxpr/ppermute | solution.py:17
  750.1 12.3 %collective-permute-start = (f32[128,256]{0,1:T(8,128)S(1)}, f32[128,256]{0,1:T(8,128)S(1)}, u32[]{:S(2)}, u32[]{:S(2)}) collective-permute-start(f32[128,256]{0,1:T(8,128)S(1)} %fusion.225), channel_id=1, source_target_pairs={{0,16},{16,32},{32,48},{48,64},{64,80},{80,96},{96,112},{112,128},... | collective-permute-start | bytes 393224 | tf_op jit(solution)/shard_map/while/body/eval_jaxpr/ppermute | solution.py:11
  (9 other events, 209.8 us)
Sparse Core Ops, SparseCore 0:
  10.0 77.3 all-gather.2
  90.8 90.4 all-gather.4
  768.2 149.0 reduce-scatter.1
where the time goes:
time: 931 us; the launch traced here: 925 us
  waiting for transfers between devices  322 us (35%)
  starting transfers between devices  223 us (24%)
  matrix products  181 us (19%)
  other arithmetic  173 us (19%)
  between operations  13.8 us (1%)
    ppermute x32, starting transfers between devices, from_behind(): return lax.ppermute(value, axis, pairs)  159 us
    reduce_scatter x1, waiting for transfers between devices, body(): lax.psum_scatter(filter_terms.reshape(blocks * rows, chans), 'ctx', scatt...  148 us
    dot_general x131, matrix products, matmul(): jnp.dot(left, right, precision=lax.Precision.HIGHEST, preferred_element_t...  129 us
    all_gather x1, waiting for transfers between devices, body(): whole_filter = lax.all_gather(filter_taps, 'ctx', axis=0, tiled=True)  89.1 us
    all_gather x1, waiting for transfers between devices, body(): lax.all_gather(out_grad, 'tp', axis=1, tiled=True)  76.7 us
    scatter-add x32, other arithmetic, add_lags(): filter_terms = filter_terms.at[step].add(lagged[:rows] * active)  72.8 us
    scatter-add x32, other arithmetic, add_lags(): filter_terms.at[jnp.maximum(step - 1, 0)]  70 us
    ppermute x32, starting transfers between devices, passed_along(): return lax.ppermute(block, axis, route)  64.1 us
  transfers between devices with their start and end apart: 67, of which 8 were waited for; matrix products, arithmetic and copies ran while one was open for 37% of the time, Pallas kernels for 0%

commit v1 on v0

--- a/solution.py
+++ b/solution.py
@@ -106,7 +106,9 @@
     dq_grad = (d_gated * saved_conv.astype(jnp.float32)).astype(jnp.bfloat16)
     dz_local = d_gated * q_proj.astype(jnp.float32)
     gated = (k_proj.astype(jnp.float32) * v_proj.astype(jnp.float32)).astype(jnp.bfloat16)
-    whole_filter = lax.all_gather(filter_taps, "ctx", axis=0, tiled=True)
+    whole_filter = jnp.concatenate(
+        lax.all_to_all(jnp.stack([filter_taps] * lax.axis_size("ctx")), "ctx", 0, 0), axis=0
+    )
     filter_blocks = whole_filter.reshape(blocks, rows, chans)
     cos_upper, cos_lower = split_table(tables[0])
     sin_upper, sin_lower = split_table(tables[1])

time: 931 us -> 893 us (0.959)
  waiting for transfers between devices: 322 us -> 252 us
  starting transfers between devices: 223 us -> 254 us
    all_gather x1 -> x0, waiting for transfers between devices: 89.1 us -> none  [body(): whole_filter = lax.all_gather(filter_taps, 'ctx', axis=0, tiled=True)]
    ppermute x32, starting transfers between devices: 159 us -> 179 us  [from_behind(): return lax.ppermute(value, axis, pairs)]
    all_gather x1, waiting for transfers between devices: 76.7 us -> 96.2 us  [body(): lax.all_gather(out_grad, 'tp', axis=1, tiled=True)]
    all_to_all x0 -> x1, starting transfers between devices: none -> 16.2 us  [body(): lax.all_to_all(jnp.stack([filter_taps] * lax.axis_size('ctx')), 'ctx', 0, 0)]
  transfers between devices with their start and end apart: 67 -> 67, of which waited for: 8 -> 7; matrix products, arithmetic and copies ran while one was open for 37% -> 38% of each run, Pallas kernels for 0% -> 0%
where the time goes in v1:
time: 893 us; the launch traced here: 887 us
  starting transfers between devices  254 us (28%)
  waiting for transfers between devices  252 us (28%)
  matrix products  185 us (21%)
  other arithmetic  168 us (19%)
  between operations  14.2 us (2%)
  local copies, waits for them, and re-layouts  11 us (1%)
    ppermute x32, starting transfers between devices, from_behind(): return lax.ppermute(value, axis, pairs)  179 us
    reduce_scatter x1, waiting for transfers between devices, body(): lax.psum_scatter(filter_terms.reshape(blocks * rows, chans), 'ctx', scatt...  147 us
    dot_general x131, matrix products, matmul(): jnp.dot(left, right, precision=lax.Precision.HIGHEST, preferred_element_t...  128 us
    all_gather x1, waiting for transfers between devices, body(): lax.all_gather(out_grad, 'tp', axis=1, tiled=True)  96.2 us
    scatter-add x32, other arithmetic, add_lags(): filter_terms.at[jnp.maximum(step - 1, 0)]  70.2 us
    scatter-add x32, other arithmetic, add_lags(): filter_terms = filter_terms.at[step].add(lagged[:rows] * active)  69.8 us
    ppermute x32, starting transfers between devices, passed_along(): return lax.ppermute(block, axis, route)  59 us
    dot_general x64, matrix products, half_matmul(): jnp.dot(lower, signal, preferred_element_type=jnp.float32)  25.2 us
  transfers between devices with their start and end apart: 67, of which 7 were waited for; matrix products, arithmetic and copies ran while one was open for 38% of the time, Pallas kernels for 0%

profile of v1, /device:TPU:2, one launch (start us, length us, event | category | flops | bytes accessed | tf_op | source)
XLA Modules:
  0.0 887.4 jit_solution(7281938196282652542)
XLA Ops:
  7.2 2.6 stack.2
  9.8 16.2 %all-to-all-start = ((bf16[32,128,256]{2,1,0:T(8,128)(2,1)}), bf16[32,128,256]{2,1,0:T(8,128)(2,1)}, u32[]{:S(2)}, u32[]{:S(2)}) async-start(bf16[32,128,256]{2,1,0:T(8,128)(2,1)} %stack.2), calls=%async_computation | async-start | bytes 4194304 | tf_op jit(solution)/shard_map/all_to_all | solution.py:110
  27.9 96.2 %all-gather.2.cloned.1.call-done = bf16[128,4096]{1,0:T(8,128)(2,1)} async-done(((bf16[128,256]{1,0:T(8,128)(2,1)}), bf16[128,4096]{1,0:T(8,128)(2,1)}) %all-gather.2.cloned.1.call-update) | async-done | bytes 1048592 | tf_op jit(solution)/shard_map/all_gather | solution.py:101
  124.1 2.7 multiply_convert_fusion
  130.1 2.3 fusion.106
  132.4 4.5 add_bitcast_fusion
  136.9 2.3 fusion.108
  139.2 4.5 add_bitcast_fusion.1
  143.7 2.5 broadcast_in_dim.41
  146.2 579.5 %while.23 = (s32[]{:T(128)}, f32[128,256]{0,1:T(8,128)S(1)}, bf16[128,256]{1,0:T(8,128)(2,1)S(1)}, f32[32,128,256]{1,2,0:T(8,128)}, s32[]{:T(128)}, /*index=5*/f...) while((s32[]{:T(128)}, f32[128,256]{0,1:T(8,128)S(1)}, ...), condition=%wide.region_3.4_spmd.clone.clone, body=%wide.region_0.3_spmd.clone.clone.sunk | while | flops 337464864 | bytes 7294348 | solution.py:155
  150.8 6.4 collective-permute-start
  162.1 2.2 fusion.231
  169.6 4.2 collective-permute-start
  178.7 2.2 fusion.231
  187.3 2.8 collective-permute-start
  194.9 2.2 fusion.231
  197.1 3.2 collective-permute-done
  204.9 6.2 collective-permute-start
  216.0 2.2 fusion.231
  223.5 7.9 collective-permute-start
  243.7 5.4 collective-permute-start
  254.0 2.2 fusion.231
  261.7 4.0 collective-permute-start
  270.6 2.2 fusion.231
  279.3 16.1 %collective-permute-start = (f32[128,256]{0,1:T(8,128)S(1)}, f32[128,256]{0,1:T(8,128)S(1)}, u32[]{:S(2)}, u32[]{:S(2)}) collective-permute-start(f32[128,256]{0,1:T(8,128)S(1)} %fusion.225), channel_id=1, source_target_pairs={{0,16},{16,32},{32,48},{48,64},{64,80},{80,96},{96,112},{112,128},... | collective-permute-start | bytes 393224 | tf_op jit(solution)/shard_map/while/body/eval_jaxpr/ppermute | solution.py:11
  307.8 5.3 collective-permute-start
  318.0 2.2 fusion.231
  325.4 6.1 collective-permute-start
  336.4 2.2 fusion.231
  343.8 5.3 collective-permute-start
  354.0 2.2 fusion.231
  361.5 5.2 collective-permute-start
  379.0 5.2 collective-permute-start
  396.5 5.2 collective-permute-start
  406.6 2.2 fusion.231
  414.0 5.2 collective-permute-start
  424.1 2.2 fusion.231
  431.6 5.2 collective-permute-start
  449.1 5.2 collective-permute-start
  459.2 2.2 fusion.231
  466.6 5.2 collective-permute-start
  484.1 5.2 collective-permute-start
  494.2 2.2 fusion.231
  501.7 5.2 collective-permute-start
  519.2 5.2 collective-permute-start
  529.3 2.2 fusion.231
  536.7 5.2 collective-permute-start
  554.3 5.2 collective-permute-start
  564.3 2.2 fusion.231
  571.8 5.2 collective-permute-start
  589.5 5.2 collective-permute-start
  607.1 5.2 collective-permute-start
  619.5 2.8 collective-permute-start.1
  625.5 5.3 collective-permute-start
  643.2 5.2 collective-permute-start
  660.7 5.2 collective-permute-start
  670.8 2.2 fusion.231
  678.3 5.2 collective-permute-start
  688.4 2.2 fusion.231
  695.8 5.2 collective-permute-start
  705.9 2.2 fusion.231
  713.4 5.2 collective-permute-start
  725.7 5.6 copy.13
  732.1 146.9 %reduce-scatter.2.cloned.1.call-done = f32[128,256]{1,0:T(8,128)} async-done(((f32[4096,256]{1,0:T(8,128)}), f32[128,256]{1,0:T(8,128)}) %reduce-scatter.2.cloned.1.call-update) | async-done | bytes 131088 | tf_op jit(solution)/shard_map/reduce_scatter | solution.py:158
  (653 shorter events, 359.5 us)
Async XLA Ops:
  9.8 118.3 %all-to-all-start = ((bf16[32,128,256]{2,1,0:T(8,128)(2,1)}), bf16[32,128,256]{2,1,0:T(8,128)(2,1)}, u32[]{:S(2)}, u32[]{:S(2)}) async-start(bf16[32,128,256]{2,1,0:T(8,128)(2,1)} %stack.2), calls=%async_computation | async-start | bytes 4194304 | tf_op jit(solution)/shard_map/all_to_all | solution.py:110
  26.0 98.1 %all-gather.2.cloned.1.call-start = ((), (), s32[]{:S(2)}) async-start(), calls=%async_computation.2 | async-start | bytes 1114112 | tf_op jit(solution)/shard_map/all_gather | solution.py:101
  26.7 852.3 %reduce-scatter.2.cloned.1.call-start = ((), (), s32[]{:S(2)}) async-start(), calls=%async_computation.3 | async-start | bytes 4325376 | tf_op jit(solution)/shard_map/reduce_scatter | solution.py:158
  146.2 18.1 %collective-permute-start.1 = (bf16[128,256]{1,0:T(8,128)(2,1)S(1)}, bf16[128,256]{1,0:T(8,128)(2,1)S(1)}, u32[]{:S(2)}, u32[]{:S(2)}) collective-permute-start(bf16[128,256]{1,0:T(8,128)(2,1)S(1)} %copy.25), channel_id=1, source_target_pairs={{0,16},{16,32},{32,48},{48,64},{64,80},{80,96},{96,112},{112,128},... | collective-permute-start | bytes 196616 | tf_op jit(solution)/shard_map/while/body/eval_jaxpr/ppermute | solution.py:17
  150.8 13.5 %collective-permute-start = (f32[128,256]{0,1:T(8,128)S(1)}, f32[128,256]{0,1:T(8,128)S(1)}, u32[]{:S(2)}, u32[]{:S(2)}) collective-permute-start(f32[128,256]{0,1:T(8,128)S(1)} %fusion.225), channel_id=1, source_target_pairs={{0,16},{16,32},{32,48},{48,64},{64,80},{80,96},{96,112},{112,128},... | collective-permute-start | bytes 393224 | tf_op jit(solution)/shard_map/while/body/eval_jaxpr/ppermute | solution.py:11
  164.3 16.6 %collective-permute-start.1 = (bf16[128,256]{1,0:T(8,128)(2,1)S(1)}, bf16[128,256]{1,0:T(8,128)(2,1)S(1)}, u32[]{:S(2)}, u32[]{:S(2)}) collective-permute-start(bf16[128,256]{1,0:T(8,128)(2,1)S(1)} %copy.25), channel_id=1, source_target_pairs={{0,16},{16,32},{32,48},{48,64},{64,80},{80,96},{96,112},{112,128},... | collective-permute-start | bytes 196616 | tf_op jit(solution)/shard_map/while/body/eval_jaxpr/ppermute | solution.py:17
  169.6 13.1 %collective-permute-start = (f32[128,256]{0,1:T(8,128)S(1)}, f32[128,256]{0,1:T(8,128)S(1)}, u32[]{:S(2)}, u32[]{:S(2)}) collective-permute-start(f32[128,256]{0,1:T(8,128)S(1)} %fusion.225), channel_id=1, source_target_pairs={{0,16},{16,32},{32,48},{48,64},{64,80},{80,96},{96,112},{112,128},... | collective-permute-start | bytes 393224 | tf_op jit(solution)/shard_map/while/body/eval_jaxpr/ppermute | solution.py:11
  182.7 14.4 %collective-permute-start.1 = (bf16[128,256]{1,0:T(8,128)(2,1)S(1)}, bf16[128,256]{1,0:T(8,128)(2,1)S(1)}, u32[]{:S(2)}, u32[]{:S(2)}) collective-permute-start(bf16[128,256]{1,0:T(8,128)(2,1)S(1)} %copy.25), channel_id=1, source_target_pairs={{0,16},{16,32},{32,48},{48,64},{64,80},{80,96},{96,112},{112,128},... | collective-permute-start | bytes 196616 | tf_op jit(solution)/shard_map/while/body/eval_jaxpr/ppermute | solution.py:17
  187.3 13.0 %collective-permute-start = (f32[128,256]{0,1:T(8,128)S(1)}, f32[128,256]{0,1:T(8,128)S(1)}, u32[]{:S(2)}, u32[]{:S(2)}) collective-permute-start(f32[128,256]{0,1:T(8,128)S(1)} %fusion.225), channel_id=1, source_target_pairs={{0,16},{16,32},{32,48},{48,64},{64,80},{80,96},{96,112},{112,128},... | collective-permute-start | bytes 393224 | tf_op jit(solution)/shard_map/while/body/eval_jaxpr/ppermute | solution.py:11
  200.3 17.9 %collective-permute-start.1 = (bf16[128,256]{1,0:T(8,128)(2,1)S(1)}, bf16[128,256]{1,0:T(8,128)(2,1)S(1)}, u32[]{:S(2)}, u32[]{:S(2)}) collective-permute-start(bf16[128,256]{1,0:T(8,128)(2,1)S(1)} %copy.25), channel_id=1, source_target_pairs={{0,16},{16,32},{32,48},{48,64},{64,80},{80,96},{96,112},{112,128},... | collective-permute-start | bytes 196616 | tf_op jit(solution)/shard_map/while/body/eval_jaxpr/ppermute | solution.py:17
  204.9 13.3 %collective-permute-start = (f32[128,256]{0,1:T(8,128)S(1)}, f32[128,256]{0,1:T(8,128)S(1)}, u32[]{:S(2)}, u32[]{:S(2)}) collective-permute-start(f32[128,256]{0,1:T(8,128)S(1)} %fusion.225), channel_id=1, source_target_pairs={{0,16},{16,32},{32,48},{48,64},{64,80},{80,96},{96,112},{112,128},... | collective-permute-start | bytes 393224 | tf_op jit(solution)/shard_map/while/body/eval_jaxpr/ppermute | solution.py:11
  218.2 20.2 %collective-permute-start.1 = (bf16[128,256]{1,0:T(8,128)(2,1)S(1)}, bf16[128,256]{1,0:T(8,128)(2,1)S(1)}, u32[]{:S(2)}, u32[]{:S(2)}) collective-permute-start(bf16[128,256]{1,0:T(8,128)(2,1)S(1)} %copy.25), channel_id=1, source_target_pairs={{0,16},{16,32},{32,48},{48,64},{64,80},{80,96},{96,112},{112,128},... | collective-permute-start | bytes 196616 | tf_op jit(solution)/shard_map/while/body/eval_jaxpr/ppermute | solution.py:17
  223.5 15.0 %collective-permute-start = (f32[128,256]{0,1:T(8,128)S(1)}, f32[128,256]{0,1:T(8,128)S(1)}, u32[]{:S(2)}, u32[]{:S(2)}) collective-permute-start(f32[128,256]{0,1:T(8,128)S(1)} %fusion.225), channel_id=1, source_target_pairs={{0,16},{16,32},{32,48},{48,64},{64,80},{80,96},{96,112},{112,128},... | collective-permute-start | bytes 393224 | tf_op jit(solution)/shard_map/while/body/eval_jaxpr/ppermute | solution.py:11
  238.5 17.7 %collective-permute-start.1 = (bf16[128,256]{1,0:T(8,128)(2,1)S(1)}, bf16[128,256]{1,0:T(8,128)(2,1)S(1)}, u32[]{:S(2)}, u32[]{:S(2)}) collective-permute-start(bf16[128,256]{1,0:T(8,128)(2,1)S(1)} %copy.25), channel_id=1, source_target_pairs={{0,16},{16,32},{32,48},{48,64},{64,80},{80,96},{96,112},{112,128},... | collective-permute-start | bytes 196616 | tf_op jit(solution)/shard_map/while/body/eval_jaxpr/ppermute | solution.py:17
  243.7 13.4 %collective-permute-start = (f32[128,256]{0,1:T(8,128)S(1)}, f32[128,256]{0,1:T(8,128)S(1)}, u32[]{:S(2)}, u32[]{:S(2)}) collective-permute-start(f32[128,256]{0,1:T(8,128)S(1)} %fusion.225), channel_id=1, source_target_pairs={{0,16},{16,32},{32,48},{48,64},{64,80},{80,96},{96,112},{112,128},... | collective-permute-start | bytes 393224 | tf_op jit(solution)/shard_map/while/body/eval_jaxpr/ppermute | solution.py:11
  257.1 15.7 %collective-permute-start.1 = (bf16[128,256]{1,0:T(8,128)(2,1)S(1)}, bf16[128,256]{1,0:T(8,128)(2,1)S(1)}, u32[]{:S(2)}, u32[]{:S(2)}) collective-permute-start(bf16[128,256]{1,0:T(8,128)(2,1)S(1)} %copy.25), channel_id=1, source_target_pairs={{0,16},{16,32},{32,48},{48,64},{64,80},{80,96},{96,112},{112,128},... | collective-permute-start | bytes 196616 | tf_op jit(solution)/shard_map/while/body/eval_jaxpr/ppermute | solution.py:17
  261.7 13.0 %collective-permute-start = (f32[128,256]{0,1:T(8,128)S(1)}, f32[128,256]{0,1:T(8,128)S(1)}, u32[]{:S(2)}, u32[]{:S(2)}) collective-permute-start(f32[128,256]{0,1:T(8,128)S(1)} %fusion.225), channel_id=1, source_target_pairs={{0,16},{16,32},{32,48},{48,64},{64,80},{80,96},{96,112},{112,128},... | collective-permute-start | bytes 393224 | tf_op jit(solution)/shard_map/while/body/eval_jaxpr/ppermute | solution.py:11
  274.7 27.8 %collective-permute-start.1 = (bf16[128,256]{1,0:T(8,128)(2,1)S(1)}, bf16[128,256]{1,0:T(8,128)(2,1)S(1)}, u32[]{:S(2)}, u32[]{:S(2)}) collective-permute-start(bf16[128,256]{1,0:T(8,128)(2,1)S(1)} %copy.25), channel_id=1, source_target_pairs={{0,16},{16,32},{32,48},{48,64},{64,80},{80,96},{96,112},{112,128},... | collective-permute-start | bytes 196616 | tf_op jit(solution)/shard_map/while/body/eval_jaxpr/ppermute | solution.py:17
  279.3 23.2 %collective-permute-start = (f32[128,256]{0,1:T(8,128)S(1)}, f32[128,256]{0,1:T(8,128)S(1)}, u32[]{:S(2)}, u32[]{:S(2)}) collective-permute-start(f32[128,256]{0,1:T(8,128)S(1)} %fusion.225), channel_id=1, source_target_pairs={{0,16},{16,32},{32,48},{48,64},{64,80},{80,96},{96,112},{112,128},... | collective-permute-start | bytes 393224 | tf_op jit(solution)/shard_map/while/body/eval_jaxpr/ppermute | solution.py:11
  302.5 17.6 %collective-permute-start.1 = (bf16[128,256]{1,0:T(8,128)(2,1)S(1)}, bf16[128,256]{1,0:T(8,128)(2,1)S(1)}, u32[]{:S(2)}, u32[]{:S(2)}) collective-permute-start(bf16[128,256]{1,0:T(8,128)(2,1)S(1)} %copy.25), channel_id=1, source_target_pairs={{0,16},{16,32},{32,48},{48,64},{64,80},{80,96},{96,112},{112,128},... | collective-permute-start | bytes 196616 | tf_op jit(solution)/shard_map/while/body/eval_jaxpr/ppermute | solution.py:17
  307.8 12.4 %collective-permute-start = (f32[128,256]{0,1:T(8,128)S(1)}, f32[128,256]{0,1:T(8,128)S(1)}, u32[]{:S(2)}, u32[]{:S(2)}) collective-permute-start(f32[128,256]{0,1:T(8,128)S(1)} %fusion.225), channel_id=1, source_target_pairs={{0,16},{16,32},{32,48},{48,64},{64,80},{80,96},{96,112},{112,128},... | collective-permute-start | bytes 393224 | tf_op jit(solution)/shard_map/while/body/eval_jaxpr/ppermute | solution.py:11
  320.2 18.4 %collective-permute-start.1 = (bf16[128,256]{1,0:T(8,128)(2,1)S(1)}, bf16[128,256]{1,0:T(8,128)(2,1)S(1)}, u32[]{:S(2)}, u32[]{:S(2)}) collective-permute-start(bf16[128,256]{1,0:T(8,128)(2,1)S(1)} %copy.25), channel_id=1, source_target_pairs={{0,16},{16,32},{32,48},{48,64},{64,80},{80,96},{96,112},{112,128},... | collective-permute-start | bytes 196616 | tf_op jit(solution)/shard_map/while/body/eval_jaxpr/ppermute | solution.py:17
  325.4 13.3 %collective-permute-start = (f32[128,256]{0,1:T(8,128)S(1)}, f32[128,256]{0,1:T(8,128)S(1)}, u32[]{:S(2)}, u32[]{:S(2)}) collective-permute-start(f32[128,256]{0,1:T(8,128)S(1)} %fusion.225), channel_id=1, source_target_pairs={{0,16},{16,32},{32,48},{48,64},{64,80},{80,96},{96,112},{112,128},... | collective-permute-start | bytes 393224 | tf_op jit(solution)/shard_map/while/body/eval_jaxpr/ppermute | solution.py:11
  338.7 17.5 %collective-permute-start.1 = (bf16[128,256]{1,0:T(8,128)(2,1)S(1)}, bf16[128,256]{1,0:T(8,128)(2,1)S(1)}, u32[]{:S(2)}, u32[]{:S(2)}) collective-permute-start(bf16[128,256]{1,0:T(8,128)(2,1)S(1)} %copy.25), channel_id=1, source_target_pairs={{0,16},{16,32},{32,48},{48,64},{64,80},{80,96},{96,112},{112,128},... | collective-permute-start | bytes 196616 | tf_op jit(solution)/shard_map/while/body/eval_jaxpr/ppermute | solution.py:17
  343.8 12.4 %collective-permute-start = (f32[128,256]{0,1:T(8,128)S(1)}, f32[128,256]{0,1:T(8,128)S(1)}, u32[]{:S(2)}, u32[]{:S(2)}) collective-permute-start(f32[128,256]{0,1:T(8,128)S(1)} %fusion.225), channel_id=1, source_target_pairs={{0,16},{16,32},{32,48},{48,64},{64,80},{80,96},{96,112},{112,128},... | collective-permute-start | bytes 393224 | tf_op jit(solution)/shard_map/while/body/eval_jaxpr/ppermute | solution.py:11
  356.2 17.5 %collective-permute-start.1 = (bf16[128,256]{1,0:T(8,128)(2,1)S(1)}, bf16[128,256]{1,0:T(8,128)(2,1)S(1)}, u32[]{:S(2)}, u32[]{:S(2)}) collective-permute-start(bf16[128,256]{1,0:T(8,128)(2,1)S(1)} %copy.25), channel_id=1, source_target_pairs={{0,16},{16,32},{32,48},{48,64},{64,80},{80,96},{96,112},{112,128},... | collective-permute-start | bytes 196616 | tf_op jit(solution)/shard_map/while/body/eval_jaxpr/ppermute | solution.py:17
  361.5 12.3 %collective-permute-start = (f32[128,256]{0,1:T(8,128)S(1)}, f32[128,256]{0,1:T(8,128)S(1)}, u32[]{:S(2)}, u32[]{:S(2)}) collective-permute-start(f32[128,256]{0,1:T(8,128)S(1)} %fusion.225), channel_id=1, source_target_pairs={{0,16},{16,32},{32,48},{48,64},{64,80},{80,96},{96,112},{112,128},... | collective-permute-start | bytes 393224 | tf_op jit(solution)/shard_map/while/body/eval_jaxpr/ppermute | solution.py:11
  373.8 17.5 %collective-permute-start.1 = (bf16[128,256]{1,0:T(8,128)(2,1)S(1)}, bf16[128,256]{1,0:T(8,128)(2,1)S(1)}, u32[]{:S(2)}, u32[]{:S(2)}) collective-permute-start(bf16[128,256]{1,0:T(8,128)(2,1)S(1)} %copy.25), channel_id=1, source_target_pairs={{0,16},{16,32},{32,48},{48,64},{64,80},{80,96},{96,112},{112,128},... | collective-permute-start | bytes 196616 | tf_op jit(solution)/shard_map/while/body/eval_jaxpr/ppermute | solution.py:17
  379.0 12.3 %collective-permute-start = (f32[128,256]{0,1:T(8,128)S(1)}, f32[128,256]{0,1:T(8,128)S(1)}, u32[]{:S(2)}, u32[]{:S(2)}) collective-permute-start(f32[128,256]{0,1:T(8,128)S(1)} %fusion.225), channel_id=1, source_target_pairs={{0,16},{16,32},{32,48},{48,64},{64,80},{80,96},{96,112},{112,128},... | collective-permute-start | bytes 393224 | tf_op jit(solution)/shard_map/while/body/eval_jaxpr/ppermute | solution.py:11
  391.3 17.5 %collective-permute-start.1 = (bf16[128,256]{1,0:T(8,128)(2,1)S(1)}, bf16[128,256]{1,0:T(8,128)(2,1)S(1)}, u32[]{:S(2)}, u32[]{:S(2)}) collective-permute-start(bf16[128,256]{1,0:T(8,128)(2,1)S(1)} %copy.25), channel_id=1, source_target_pairs={{0,16},{16,32},{32,48},{48,64},{64,80},{80,96},{96,112},{112,128},... | collective-permute-start | bytes 196616 | tf_op jit(solution)/shard_map/while/body/eval_jaxpr/ppermute | solution.py:17
  396.5 12.3 %collective-permute-start = (f32[128,256]{0,1:T(8,128)S(1)}, f32[128,256]{0,1:T(8,128)S(1)}, u32[]{:S(2)}, u32[]{:S(2)}) collective-permute-start(f32[128,256]{0,1:T(8,128)S(1)} %fusion.225), channel_id=1, source_target_pairs={{0,16},{16,32},{32,48},{48,64},{64,80},{80,96},{96,112},{112,128},... | collective-permute-start | bytes 393224 | tf_op jit(solution)/shard_map/while/body/eval_jaxpr/ppermute | solution.py:11
  408.8 17.5 %collective-permute-start.1 = (bf16[128,256]{1,0:T(8,128)(2,1)S(1)}, bf16[128,256]{1,0:T(8,128)(2,1)S(1)}, u32[]{:S(2)}, u32[]{:S(2)}) collective-permute-start(bf16[128,256]{1,0:T(8,128)(2,1)S(1)} %copy.25), channel_id=1, source_target_pairs={{0,16},{16,32},{32,48},{48,64},{64,80},{80,96},{96,112},{112,128},... | collective-permute-start | bytes 196616 | tf_op jit(solution)/shard_map/while/body/eval_jaxpr/ppermute | solution.py:17
  414.0 12.3 %collective-permute-start = (f32[128,256]{0,1:T(8,128)S(1)}, f32[128,256]{0,1:T(8,128)S(1)}, u32[]{:S(2)}, u32[]{:S(2)}) collective-permute-start(f32[128,256]{0,1:T(8,128)S(1)} %fusion.225), channel_id=1, source_target_pairs={{0,16},{16,32},{32,48},{48,64},{64,80},{80,96},{96,112},{112,128},... | collective-permute-start | bytes 393224 | tf_op jit(solution)/shard_map/while/body/eval_jaxpr/ppermute | solution.py:11
  426.3 17.5 %collective-permute-start.1 = (bf16[128,256]{1,0:T(8,128)(2,1)S(1)}, bf16[128,256]{1,0:T(8,128)(2,1)S(1)}, u32[]{:S(2)}, u32[]{:S(2)}) collective-permute-start(bf16[128,256]{1,0:T(8,128)(2,1)S(1)} %copy.25), channel_id=1, source_target_pairs={{0,16},{16,32},{32,48},{48,64},{64,80},{80,96},{96,112},{112,128},... | collective-permute-start | bytes 196616 | tf_op jit(solution)/shard_map/while/body/eval_jaxpr/ppermute | solution.py:17
  431.6 12.3 %collective-permute-start = (f32[128,256]{0,1:T(8,128)S(1)}, f32[128,256]{0,1:T(8,128)S(1)}, u32[]{:S(2)}, u32[]{:S(2)}) collective-permute-start(f32[128,256]{0,1:T(8,128)S(1)} %fusion.225), channel_id=1, source_target_pairs={{0,16},{16,32},{32,48},{48,64},{64,80},{80,96},{96,112},{112,128},... | collective-permute-start | bytes 393224 | tf_op jit(solution)/shard_map/while/body/eval_jaxpr/ppermute | solution.py:11
  443.9 17.5 %collective-permute-start.1 = (bf16[128,256]{1,0:T(8,128)(2,1)S(1)}, bf16[128,256]{1,0:T(8,128)(2,1)S(1)}, u32[]{:S(2)}, u32[]{:S(2)}) collective-permute-start(bf16[128,256]{1,0:T(8,128)(2,1)S(1)} %copy.25), channel_id=1, source_target_pairs={{0,16},{16,32},{32,48},{48,64},{64,80},{80,96},{96,112},{112,128},... | collective-permute-start | bytes 196616 | tf_op jit(solution)/shard_map/while/body/eval_jaxpr/ppermute | solution.py:17
  449.1 12.3 %collective-permute-start = (f32[128,256]{0,1:T(8,128)S(1)}, f32[128,256]{0,1:T(8,128)S(1)}, u32[]{:S(2)}, u32[]{:S(2)}) collective-permute-start(f32[128,256]{0,1:T(8,128)S(1)} %fusion.225), channel_id=1, source_target_pairs={{0,16},{16,32},{32,48},{48,64},{64,80},{80,96},{96,112},{112,128},... | collective-permute-start | bytes 393224 | tf_op jit(solution)/shard_map/while/body/eval_jaxpr/ppermute | solution.py:11
  461.4 17.5 %collective-permute-start.1 = (bf16[128,256]{1,0:T(8,128)(2,1)S(1)}, bf16[128,256]{1,0:T(8,128)(2,1)S(1)}, u32[]{:S(2)}, u32[]{:S(2)}) collective-permute-start(bf16[128,256]{1,0:T(8,128)(2,1)S(1)} %copy.25), channel_id=1, source_target_pairs={{0,16},{16,32},{32,48},{48,64},{64,80},{80,96},{96,112},{112,128},... | collective-permute-start | bytes 196616 | tf_op jit(solution)/shard_map/while/body/eval_jaxpr/ppermute | solution.py:17
  466.6 12.3 %collective-permute-start = (f32[128,256]{0,1:T(8,128)S(1)}, f32[128,256]{0,1:T(8,128)S(1)}, u32[]{:S(2)}, u32[]{:S(2)}) collective-permute-start(f32[128,256]{0,1:T(8,128)S(1)} %fusion.225), channel_id=1, source_target_pairs={{0,16},{16,32},{32,48},{48,64},{64,80},{80,96},{96,112},{112,128},... | collective-permute-start | bytes 393224 | tf_op jit(solution)/shard_map/while/body/eval_jaxpr/ppermute | solution.py:11
  478.9 17.5 %collective-permute-start.1 = (bf16[128,256]{1,0:T(8,128)(2,1)S(1)}, bf16[128,256]{1,0:T(8,128)(2,1)S(1)}, u32[]{:S(2)}, u32[]{:S(2)}) collective-permute-start(bf16[128,256]{1,0:T(8,128)(2,1)S(1)} %copy.25), channel_id=1, source_target_pairs={{0,16},{16,32},{32,48},{48,64},{64,80},{80,96},{96,112},{112,128},... | collective-permute-start | bytes 196616 | tf_op jit(solution)/shard_map/while/body/eval_jaxpr/ppermute | solution.py:17
  484.1 12.3 %collective-permute-start = (f32[128,256]{0,1:T(8,128)S(1)}, f32[128,256]{0,1:T(8,128)S(1)}, u32[]{:S(2)}, u32[]{:S(2)}) collective-permute-start(f32[128,256]{0,1:T(8,128)S(1)} %fusion.225), channel_id=1, source_target_pairs={{0,16},{16,32},{32,48},{48,64},{64,80},{80,96},{96,112},{112,128},... | collective-permute-start | bytes 393224 | tf_op jit(solution)/shard_map/while/body/eval_jaxpr/ppermute | solution.py:11
  496.5 17.5 %collective-permute-start.1 = (bf16[128,256]{1,0:T(8,128)(2,1)S(1)}, bf16[128,256]{1,0:T(8,128)(2,1)S(1)}, u32[]{:S(2)}, u32[]{:S(2)}) collective-permute-start(bf16[128,256]{1,0:T(8,128)(2,1)S(1)} %copy.25), channel_id=1, source_target_pairs={{0,16},{16,32},{32,48},{48,64},{64,80},{80,96},{96,112},{112,128},... | collective-permute-start | bytes 196616 | tf_op jit(solution)/shard_map/while/body/eval_jaxpr/ppermute | solution.py:17
  501.7 12.3 %collective-permute-start = (f32[128,256]{0,1:T(8,128)S(1)}, f32[128,256]{0,1:T(8,128)S(1)}, u32[]{:S(2)}, u32[]{:S(2)}) collective-permute-start(f32[128,256]{0,1:T(8,128)S(1)} %fusion.225), channel_id=1, source_target_pairs={{0,16},{16,32},{32,48},{48,64},{64,80},{80,96},{96,112},{112,128},... | collective-permute-start | bytes 393224 | tf_op jit(solution)/shard_map/while/body/eval_jaxpr/ppermute | solution.py:11
  514.0 17.5 %collective-permute-start.1 = (bf16[128,256]{1,0:T(8,128)(2,1)S(1)}, bf16[128,256]{1,0:T(8,128)(2,1)S(1)}, u32[]{:S(2)}, u32[]{:S(2)}) collective-permute-start(bf16[128,256]{1,0:T(8,128)(2,1)S(1)} %copy.25), channel_id=1, source_target_pairs={{0,16},{16,32},{32,48},{48,64},{64,80},{80,96},{96,112},{112,128},... | collective-permute-start | bytes 196616 | tf_op jit(solution)/shard_map/while/body/eval_jaxpr/ppermute | solution.py:17
  519.2 12.3 %collective-permute-start = (f32[128,256]{0,1:T(8,128)S(1)}, f32[128,256]{0,1:T(8,128)S(1)}, u32[]{:S(2)}, u32[]{:S(2)}) collective-permute-start(f32[128,256]{0,1:T(8,128)S(1)} %fusion.225), channel_id=1, source_target_pairs={{0,16},{16,32},{32,48},{48,64},{64,80},{80,96},{96,112},{112,128},... | collective-permute-start | bytes 393224 | tf_op jit(solution)/shard_map/while/body/eval_jaxpr/ppermute | solution.py:11
  531.5 17.5 %collective-permute-start.1 = (bf16[128,256]{1,0:T(8,128)(2,1)S(1)}, bf16[128,256]{1,0:T(8,128)(2,1)S(1)}, u32[]{:S(2)}, u32[]{:S(2)}) collective-permute-start(bf16[128,256]{1,0:T(8,128)(2,1)S(1)} %copy.25), channel_id=1, source_target_pairs={{0,16},{16,32},{32,48},{48,64},{64,80},{80,96},{96,112},{112,128},... | collective-permute-start | bytes 196616 | tf_op jit(solution)/shard_map/while/body/eval_jaxpr/ppermute | solution.py:17
  536.7 12.3 %collective-permute-start = (f32[128,256]{0,1:T(8,128)S(1)}, f32[128,256]{0,1:T(8,128)S(1)}, u32[]{:S(2)}, u32[]{:S(2)}) collective-permute-start(f32[128,256]{0,1:T(8,128)S(1)} %fusion.225), channel_id=1, source_target_pairs={{0,16},{16,32},{32,48},{48,64},{64,80},{80,96},{96,112},{112,128},... | collective-permute-start | bytes 393224 | tf_op jit(solution)/shard_map/while/body/eval_jaxpr/ppermute | solution.py:11
  549.0 17.5 %collective-permute-start.1 = (bf16[128,256]{1,0:T(8,128)(2,1)S(1)}, bf16[128,256]{1,0:T(8,128)(2,1)S(1)}, u32[]{:S(2)}, u32[]{:S(2)}) collective-permute-start(bf16[128,256]{1,0:T(8,128)(2,1)S(1)} %copy.25), channel_id=1, source_target_pairs={{0,16},{16,32},{32,48},{48,64},{64,80},{80,96},{96,112},{112,128},... | collective-permute-start | bytes 196616 | tf_op jit(solution)/shard_map/while/body/eval_jaxpr/ppermute | solution.py:17
  554.3 12.3 %collective-permute-start = (f32[128,256]{0,1:T(8,128)S(1)}, f32[128,256]{0,1:T(8,128)S(1)}, u32[]{:S(2)}, u32[]{:S(2)}) collective-permute-start(f32[128,256]{0,1:T(8,128)S(1)} %fusion.225), channel_id=1, source_target_pairs={{0,16},{16,32},{32,48},{48,64},{64,80},{80,96},{96,112},{112,128},... | collective-permute-start | bytes 393224 | tf_op jit(solution)/shard_map/while/body/eval_jaxpr/ppermute | solution.py:11
  566.6 17.5 %collective-permute-start.1 = (bf16[128,256]{1,0:T(8,128)(2,1)S(1)}, bf16[128,256]{1,0:T(8,128)(2,1)S(1)}, u32[]{:S(2)}, u32[]{:S(2)}) collective-permute-start(bf16[128,256]{1,0:T(8,128)(2,1)S(1)} %copy.25), channel_id=1, source_target_pairs={{0,16},{16,32},{32,48},{48,64},{64,80},{80,96},{96,112},{112,128},... | collective-permute-start | bytes 196616 | tf_op jit(solution)/shard_map/while/body/eval_jaxpr/ppermute | solution.py:17
  584.1 17.7 %collective-permute-start.1 = (bf16[128,256]{1,0:T(8,128)(2,1)S(1)}, bf16[128,256]{1,0:T(8,128)(2,1)S(1)}, u32[]{:S(2)}, u32[]{:S(2)}) collective-permute-start(bf16[128,256]{1,0:T(8,128)(2,1)S(1)} %copy.25), channel_id=1, source_target_pairs={{0,16},{16,32},{32,48},{48,64},{64,80},{80,96},{96,112},{112,128},... | collective-permute-start | bytes 196616 | tf_op jit(solution)/shard_map/while/body/eval_jaxpr/ppermute | solution.py:17
  589.5 12.3 %collective-permute-start = (f32[128,256]{0,1:T(8,128)S(1)}, f32[128,256]{0,1:T(8,128)S(1)}, u32[]{:S(2)}, u32[]{:S(2)}) collective-permute-start(f32[128,256]{0,1:T(8,128)S(1)} %fusion.225), channel_id=1, source_target_pairs={{0,16},{16,32},{32,48},{48,64},{64,80},{80,96},{96,112},{112,128},... | collective-permute-start | bytes 393224 | tf_op jit(solution)/shard_map/while/body/eval_jaxpr/ppermute | solution.py:11
  601.9 17.6 %collective-permute-start.1 = (bf16[128,256]{1,0:T(8,128)(2,1)S(1)}, bf16[128,256]{1,0:T(8,128)(2,1)S(1)}, u32[]{:S(2)}, u32[]{:S(2)}) collective-permute-start(bf16[128,256]{1,0:T(8,128)(2,1)S(1)} %copy.25), channel_id=1, source_target_pairs={{0,16},{16,32},{32,48},{48,64},{64,80},{80,96},{96,112},{112,128},... | collective-permute-start | bytes 196616 | tf_op jit(solution)/shard_map/while/body/eval_jaxpr/ppermute | solution.py:17
  607.1 12.3 %collective-permute-start = (f32[128,256]{0,1:T(8,128)S(1)}, f32[128,256]{0,1:T(8,128)S(1)}, u32[]{:S(2)}, u32[]{:S(2)}) collective-permute-start(f32[128,256]{0,1:T(8,128)S(1)} %fusion.225), channel_id=1, source_target_pairs={{0,16},{16,32},{32,48},{48,64},{64,80},{80,96},{96,112},{112,128},... | collective-permute-start | bytes 393224 | tf_op jit(solution)/shard_map/while/body/eval_jaxpr/ppermute | solution.py:11
  619.5 18.5 %collective-permute-start.1 = (bf16[128,256]{1,0:T(8,128)(2,1)S(1)}, bf16[128,256]{1,0:T(8,128)(2,1)S(1)}, u32[]{:S(2)}, u32[]{:S(2)}) collective-permute-start(bf16[128,256]{1,0:T(8,128)(2,1)S(1)} %copy.25), channel_id=1, source_target_pairs={{0,16},{16,32},{32,48},{48,64},{64,80},{80,96},{96,112},{112,128},... | collective-permute-start | bytes 196616 | tf_op jit(solution)/shard_map/while/body/eval_jaxpr/ppermute | solution.py:17
  625.5 12.4 %collective-permute-start = (f32[128,256]{0,1:T(8,128)S(1)}, f32[128,256]{0,1:T(8,128)S(1)}, u32[]{:S(2)}, u32[]{:S(2)}) collective-permute-start(f32[128,256]{0,1:T(8,128)S(1)} %fusion.225), channel_id=1, source_target_pairs={{0,16},{16,32},{32,48},{48,64},{64,80},{80,96},{96,112},{112,128},... | collective-permute-start | bytes 393224 | tf_op jit(solution)/shard_map/while/body/eval_jaxpr/ppermute | solution.py:11
  637.9 17.5 %collective-permute-start.1 = (bf16[128,256]{1,0:T(8,128)(2,1)S(1)}, bf16[128,256]{1,0:T(8,128)(2,1)S(1)}, u32[]{:S(2)}, u32[]{:S(2)}) collective-permute-start(bf16[128,256]{1,0:T(8,128)(2,1)S(1)} %copy.25), channel_id=1, source_target_pairs={{0,16},{16,32},{32,48},{48,64},{64,80},{80,96},{96,112},{112,128},... | collective-permute-start | bytes 196616 | tf_op jit(solution)/shard_map/while/body/eval_jaxpr/ppermute | solution.py:17
  643.2 12.3 %collective-permute-start = (f32[128,256]{0,1:T(8,128)S(1)}, f32[128,256]{0,1:T(8,128)S(1)}, u32[]{:S(2)}, u32[]{:S(2)}) collective-permute-start(f32[128,256]{0,1:T(8,128)S(1)} %fusion.225), channel_id=1, source_target_pairs={{0,16},{16,32},{32,48},{48,64},{64,80},{80,96},{96,112},{112,128},... | collective-permute-start | bytes 393224 | tf_op jit(solution)/shard_map/while/body/eval_jaxpr/ppermute | solution.py:11
  655.5 17.5 %collective-permute-start.1 = (bf16[128,256]{1,0:T(8,128)(2,1)S(1)}, bf16[128,256]{1,0:T(8,128)(2,1)S(1)}, u32[]{:S(2)}, u32[]{:S(2)}) collective-permute-start(bf16[128,256]{1,0:T(8,128)(2,1)S(1)} %copy.25), channel_id=1, source_target_pairs={{0,16},{16,32},{32,48},{48,64},{64,80},{80,96},{96,112},{112,128},... | collective-permute-start | bytes 196616 | tf_op jit(solution)/shard_map/while/body/eval_jaxpr/ppermute | solution.py:17
  660.7 12.3 %collective-permute-start = (f32[128,256]{0,1:T(8,128)S(1)}, f32[128,256]{0,1:T(8,128)S(1)}, u32[]{:S(2)}, u32[]{:S(2)}) collective-permute-start(f32[128,256]{0,1:T(8,128)S(1)} %fusion.225), channel_id=1, source_target_pairs={{0,16},{16,32},{32,48},{48,64},{64,80},{80,96},{96,112},{112,128},... | collective-permute-start | bytes 393224 | tf_op jit(solution)/shard_map/while/body/eval_jaxpr/ppermute | solution.py:11
  673.0 17.5 %collective-permute-start.1 = (bf16[128,256]{1,0:T(8,128)(2,1)S(1)}, bf16[128,256]{1,0:T(8,128)(2,1)S(1)}, u32[]{:S(2)}, u32[]{:S(2)}) collective-permute-start(bf16[128,256]{1,0:T(8,128)(2,1)S(1)} %copy.25), channel_id=1, source_target_pairs={{0,16},{16,32},{32,48},{48,64},{64,80},{80,96},{96,112},{112,128},... | collective-permute-start | bytes 196616 | tf_op jit(solution)/shard_map/while/body/eval_jaxpr/ppermute | solution.py:17
  678.3 12.3 %collective-permute-start = (f32[128,256]{0,1:T(8,128)S(1)}, f32[128,256]{0,1:T(8,128)S(1)}, u32[]{:S(2)}, u32[]{:S(2)}) collective-permute-start(f32[128,256]{0,1:T(8,128)S(1)} %fusion.225), channel_id=1, source_target_pairs={{0,16},{16,32},{32,48},{48,64},{64,80},{80,96},{96,112},{112,128},... | collective-permute-start | bytes 393224 | tf_op jit(solution)/shard_map/while/body/eval_jaxpr/ppermute | solution.py:11
  690.6 17.5 %collective-permute-start.1 = (bf16[128,256]{1,0:T(8,128)(2,1)S(1)}, bf16[128,256]{1,0:T(8,128)(2,1)S(1)}, u32[]{:S(2)}, u32[]{:S(2)}) collective-permute-start(bf16[128,256]{1,0:T(8,128)(2,1)S(1)} %copy.25), channel_id=1, source_target_pairs={{0,16},{16,32},{32,48},{48,64},{64,80},{80,96},{96,112},{112,128},... | collective-permute-start | bytes 196616 | tf_op jit(solution)/shard_map/while/body/eval_jaxpr/ppermute | solution.py:17
  708.1 17.5 %collective-permute-start.1 = (bf16[128,256]{1,0:T(8,128)(2,1)S(1)}, bf16[128,256]{1,0:T(8,128)(2,1)S(1)}, u32[]{:S(2)}, u32[]{:S(2)}) collective-permute-start(bf16[128,256]{1,0:T(8,128)(2,1)S(1)} %copy.25), channel_id=1, source_target_pairs={{0,16},{16,32},{32,48},{48,64},{64,80},{80,96},{96,112},{112,128},... | collective-permute-start | bytes 196616 | tf_op jit(solution)/shard_map/while/body/eval_jaxpr/ppermute | solution.py:17
  (9 other events, 430.6 us)
Sparse Core Ops, SparseCore 0:
  28.8 95.2 all-gather.1
  731.4 147.5 reduce-scatter.1
